TPU v7x, 32 devices: a whole 2x2x4 slice. The times are simulated.
32 devices in a mesh: batch: 4 (over y, x), train: 8 (over z, core).
Axes of the slice: x: 2, y: 2, z: 4, core: 2. Of those that a mesh axis runs over, the one named last changes fastest.
Arguments:
- batch_rows: int32 [2, 4096], replicated, may hold values from 0 to 32767, as said below
- train_embed: bfloat16 [32768, 256], P('train'), may hold values from -6 to 6
- lib_embed: bfloat16 [4096, 256], P('batch'), may hold values from -6 to 6
- labels: float32 [32768], P('train'), may hold values from -6 to 6
- prior_draws: float32 [32, 32768], P(None, 'train'), may hold values from -6 to 6
- noise_draws: float32 [32, 32768], P(None, 'train'), may hold values from -6 to 6
- coefficients: float32 [33, 32768], P(None, 'train'), may hold values from -4 to 4
- velocity: float32 [33, 32768], P(None, 'train'), may hold values from -1.6 to 1.6
- library_prior: float32 [32, 4096], P(None, ('batch', 'train')), may hold values from -6 to 6
Outputs:
- new_coefficients: float32 [33, 32768], P(None, 'train')
- new_velocity: float32 [33, 32768], P(None, 'train')
- predictions: float32 [33, 4096], P(None, ('batch', 'train'))
Inputs may be any that keep to these rules, and one draw needn't show every extreme that they name: `batch_rows`: each step's 4096 rows are distinct. A step's positions fall into runs of 128; run number q holds rows of the range starting at (q % 8) * 4096 of length 4096.
All inputs are finite; a program needn't handle non-finite values.
Results may differ from a plain program's by a relative error of at most 0.009.
Values may be sent and summed in bfloat16 or wider, within the bound.
A program may use at most 64 MiB of HBM per device.

v0:
```python
import functools
import math

import jax
import jax.numpy as jnp
from jax import lax
from jax.experimental import pallas as pl
from jax.experimental.pallas import tpu as pltpu
from jax.sharding import PartitionSpec as P

momentum = 0.9
step_rate = 0.1
noise_var = 0.5
noise_scale = 0.7071067811865476
length_sq = 0.088

f32 = jnp.float32
bf16 = jnp.bfloat16
BLOCK = 256


def dot(a, b):
    return lax.dot_general(a, b, (((1,), (0,)), ((), ())), preferred_element_type=f32)


def dot_t(a, b):
    return lax.dot_general(a, b, (((1,), (1,)), ((), ())), preferred_element_type=f32)


def body(
    T, B, COLS,
    rows_ref, embed_hbm, lib_hbm, labels_hbm, prior_hbm, noise_hbm, coef_hbm, vel_hbm, shift_ref,
    newc_hbm, newv_hbm, pred_ref,
    embed, lib, labels, prior, noise, coef, vel, outc, outv,
    norms, hot0, hot1, wide, targets, w_first, w_base,
    qbuf, qt, acc, acc_lib, keys0, keys1, part2, part_l0, part_l1, overlap, own_terms,
    rs_send, rs_recv, rl_send, rl_recv, ag, gall,
    in_sem, out_sem, q_send, q_recv, f_send, f_recv, rs_ss, rs_rs, ag_ss, ag_rs,
):
    t = lax.axis_index("train")
    b = lax.axis_index("batch")
    R, D = embed.shape
    CP = acc.shape[0]
    O = ag.shape[3]
    OL = rl_send.shape[2]
    H = T // 2
    hots = (hot0, hot1)
    alpha = math.sqrt(5.0 / (length_sq * D))
    gamma = alpha * math.log2(math.e)
    c1 = 1.5 / alpha
    c2 = 0.75 / (alpha * alpha)
    kappa = alpha * alpha / 3.0

    ins = []
    for i, (src, dst) in enumerate(
        (
            (embed_hbm, embed), (lib_hbm, lib), (coef_hbm, coef), (vel_hbm, vel),
            (labels_hbm, labels), (prior_hbm, prior), (noise_hbm, noise),
        )
    ):
        copy = pltpu.make_async_copy(src, dst, in_sem.at[i])
        copy.start()
        ins.append(copy)

    barrier = pltpu.get_barrier_semaphore()
    for d in range(1, T):
        pl.semaphore_signal(
            barrier, inc=1, device_id={"train": lax.rem(t + d, T)},
            device_id_type=pl.DeviceIdType.MESH,
        )
    for d in range(1, B):
        pl.semaphore_signal(
            barrier, inc=1, device_id={"batch": lax.rem(b + d, B)},
            device_id_type=pl.DeviceIdType.MESH,
        )

    base_row = (t * R).astype(f32)
    diagonal = lax.broadcasted_iota(jnp.int32, (O, O), 0) == lax.broadcasted_iota(
        jnp.int32, (O, O), 1
    )

    def build_hot(s, d):
        group = lax.rem(b + B - d, B)
        run = rows_ref[pl.ds(s * (B * T) + group * T + t, 1), :].astype(f32) - base_row
        column = jnp.sum(jnp.where(diagonal, run, 0.0), axis=1, keepdims=True).astype(jnp.int32)
        lane = lax.broadcasted_iota(jnp.int32, (O, R), 1)
        hots[s][d * O : (d + 1) * O, :] = jnp.where(column == lane, 1.0, 0.0).astype(bf16)

    def remote(src, dst, ss, rs, axis, peer):
        return pltpu.make_async_remote_copy(
            src_ref=src, dst_ref=dst, send_sem=ss, recv_sem=rs,
            device_id={axis: peer}, device_id_type=pl.DeviceIdType.MESH,
        )

    sibling = t + 1 - 2 * lax.rem(t, 2)
    sends = []

    def q_direct(s, d):
        return remote(
            qbuf.at[s, t], qbuf.at[s, t], q_send.at[s, d], q_recv.at[s, d],
            "train", lax.rem(t + 2 * d, T),
        )

    def q_direct_recv(s, d):
        slot = lax.rem(t + T - 2 * d, T)
        remote(
            qbuf.at[s, slot], qbuf.at[s, slot], q_send.at[s, d], q_recv.at[s, d],
            "train", slot,
        ).wait_recv()

    def q_forward(s, d):
        slot = lax.rem(t + T - 2 * d, T)
        return remote(
            qbuf.at[s, slot], qbuf.at[s, slot], f_send.at[s, d], f_recv.at[s, d],
            "train", sibling,
        )

    def q_forward_recv(s, d):
        slot = lax.rem(sibling + T - 2 * d, T)
        remote(
            qbuf.at[s, slot], qbuf.at[s, slot], f_send.at[s, d], f_recv.at[s, d],
            "train", sibling,
        ).wait_recv()

    def start(copy):
        copy.start()
        sends.append(copy)

    def send_queries(s):
        for d in range(1, H):
            start(q_direct(s, d))
        start(q_forward(s, 0))

    def forward_queries(s):
        for d in range(1, H):
            q_direct_recv(s, d)
            start(q_forward(s, d))

    def finish_queries(s):
        for d in range(H):
            q_forward_recv(s, d)

    build_hot(0, 0)
    build_hot(1, 0)
    ins[0].wait()
    for s in range(2):
        qbuf[s, t] = dot(hots[s][0:O, :], embed[...]).astype(bf16)
    pl.semaphore_wait(barrier, T - 1 + B - 1)
    send_queries(0)

    def norm_block(i, _):
        at = pl.ds(pl.multiple_of(i * BLOCK, BLOCK), BLOCK)
        x = embed[at, :].astype(f32)
        norms[at, :] = jnp.broadcast_to(jnp.sum(x * x, axis=1, keepdims=True), (BLOCK, 128))
        return 0

    lax.fori_loop(0, R // BLOCK, norm_block, 0)

    ins[2].wait()
    ins[3].wait()
    wide[COLS - 1 : CP, :] = jnp.zeros((CP - COLS + 1, R), f32)
    wide[0:COLS, :] = coef[...] + momentum * (1.0 + momentum) * vel[...]
    w_base[...] = wide[...].astype(bf16)

    def query_side(q):
        qf = q.astype(f32).T
        qt[...] = (-2.0 * qf).astype(bf16)
        return jnp.sum(qf * qf, axis=0, keepdims=True)

    def kernel_block(keys, key_norms, query_norms):
        Q = query_norms.shape[1]
        wide_norms = jnp.concatenate([key_norms] * (Q // 128), axis=1)
        dist = jnp.maximum(dot(keys, qt[...]) + query_norms + wide_norms, 1e-20)
        root = dist * lax.rsqrt(dist)
        shifted = root + c1
        return ((shifted * shifted + c2) * jnp.exp2(root * (-gamma))).astype(bf16)

    def apply_blocks(lower, upper, weights, query_norms, total):
        def step(i, _):
            at = pl.ds(pl.multiple_of(i * BLOCK, BLOCK), BLOCK)
            tile = kernel_block(embed[at, :], norms[at, :], query_norms)
            total[...] += dot(weights[:, at], tile)
            return 0

        lax.fori_loop(lower, upper, step, 0)

    def compact(keys, out, query_norms):
        x = keys[...].astype(f32)
        key_norms = jnp.broadcast_to(jnp.sum(x * x, axis=1, keepdims=True), (x.shape[0], 128))
        size = min(BLOCK, x.shape[0])
        for i in range(x.shape[0] // size):
            at = slice(i * size, (i + 1) * size)
            out[at, :] = kernel_block(keys[at, :], key_norms[at, :], query_norms)

    def scatter_send(ph, value):
        send, recv, size = (rs_send.at[ph], rs_recv.at[ph], O) if ph < 2 else (rl_send, rl_recv, OL)
        for k in range(T):
            send[k] = value[:, k * size : (k + 1) * size].astype(bf16)
        for d in range(1, T):
            peer = lax.rem(t + d, T)
            start(
                remote(
                    send.at[peer], recv.at[d - 1], rs_ss.at[ph, d], rs_rs.at[ph, d], "train", peer
                )
            )

    def scatter_recv(ph):
        send, recv = (rs_send.at[ph], rs_recv.at[ph]) if ph < 2 else (rl_send, rl_recv)
        total = send[t].astype(f32)
        for d in range(1, T):
            remote(
                send.at[0], recv.at[d - 1], rs_ss.at[ph, d], rs_rs.at[ph, d],
                "train", lax.rem(t + d, T),
            ).wait_recv()
            total = total + recv[d - 1].astype(f32)
        return total

    def share(ph, value):
        ag[ph, 0] = value.astype(bf16)
        for d in range(1, B):
            start(
                remote(
                    ag.at[ph, 0], ag.at[ph, d], ag_ss.at[ph, d], ag_rs.at[ph, d],
                    "batch", lax.rem(b + d, B),
                )
            )

    def collect(ph):
        for d in range(1, B):
            remote(
                ag.at[ph, 0], ag.at[ph, d], ag_ss.at[ph, d], ag_rs.at[ph, d],
                "batch", lax.rem(b + d, B),
            ).wait_recv()
        for d in range(B):
            gall[ph, :, d * O : (d + 1) * O] = ag[ph, d]

    blocks = R // BLOCK
    half = blocks // 2

    ins[1].wait()
    acc_lib[...] = jnp.zeros_like(acc_lib)
    lib_norms = query_side(lib[...])
    apply_blocks(0, half // 2, w_base, lib_norms, acc_lib)

    ins[4].wait()
    ins[5].wait()
    ins[6].wait()
    targets[COLS - 1 : CP, :] = jnp.zeros((CP - COLS + 1, R), f32)
    targets[0:1, :] = labels[...]
    targets[1:COLS, :] = labels[...] - prior[...] - noise_scale * noise[...]

    def own_term(s):
        value = noise_var * wide[...] - targets[...]
        high = value.astype(bf16)
        low = (value - high.astype(f32)).astype(bf16)
        own = hots[s][0:O, :]
        own_terms[s] = dot_t(high, own) + dot_t(low, own)

    own_term(1)
    wide[0:COLS, :] = coef[...] + momentum * vel[...]
    w_first[...] = wide[...].astype(bf16)
    own_term(0)
    for d in range(1, B):
        build_hot(0, d)
    keys0[...] = dot(hot0[...], embed[...]).astype(bf16)
    overlap[...] = dot_t(hot0[...], hot1[0:O, :]).astype(bf16)

    forward_queries(0)
    send_queries(1)
    apply_blocks(half // 2, half, w_base, lib_norms, acc_lib)
    finish_queries(0)

    acc[...] = jnp.zeros_like(acc)
    first_norms = query_side(qbuf[0].reshape(T * O, D))
    apply_blocks(0, blocks, w_first, first_norms, acc)
    scatter_send(0, kappa * acc[...])
    forward_queries(1)
    for d in range(1, B):
        build_hot(1, d)
    keys1[...] = dot(hot1[...], embed[...]).astype(bf16)
    finish_queries(1)

    acc[...] = jnp.zeros_like(acc)
    second_norms = query_side(qbuf[1].reshape(T * O, D))
    apply_blocks(0, half, w_base, second_norms, acc)
    share(0, scatter_recv(0) + own_terms[0])
    apply_blocks(half, blocks, w_base, second_norms, acc)
    compact(keys0, part2, second_norms)
    collect(0)
    g0 = gall[0]
    look = step_rate * (1.0 + momentum)
    scatter_send(1, kappa * (acc[...] - look * dot(g0, part2[...])))
    own_terms[1] = own_terms[1] - (noise_var * look) * dot(g0, overlap[...])

    lib_norms = query_side(lib[...])
    mid = half + half // 2
    apply_blocks(half, mid, w_base, lib_norms, acc_lib)
    share(1, scatter_recv(1) + own_terms[1])
    apply_blocks(mid, blocks, w_base, lib_norms, acc_lib)
    compact(keys0, part_l0, lib_norms)
    compact(keys1, part_l1, lib_norms)
    acc_lib[...] -= look * dot(g0, part_l0[...])
    collect(1)
    g1 = gall[1]
    scatter_send(2, kappa * (acc_lib[...] - step_rate * dot(g1, part_l1[...])))

    CH = min(R, 1024)
    for i in range(R // CH):
        at = slice(i * CH, (i + 1) * CH)
        grad0 = dot(g0, hot0[:, at])[0:COLS]
        grad1 = dot(g1, hot1[:, at])[0:COLS]
        v1 = momentum * vel[:, at] - step_rate * grad0
        v2 = momentum * v1 - step_rate * grad1
        outv[:, at] = v2
        outc[:, at] = (coef[:, at] + v1) + v2
    out_c = pltpu.make_async_copy(outc, newc_hbm, out_sem.at[0])
    out_v = pltpu.make_async_copy(outv, newv_hbm, out_sem.at[1])
    out_c.start()
    out_v.start()

    total = scatter_recv(2)
    pred_ref[0:1, :] = total[0:1]
    pred_ref[1:COLS, :] = total[1:COLS] + shift_ref[...]
    out_c.wait()
    out_v.wait()
    for copy in sends:
        copy.wait_send()


def per_device(
    T, B,
    batch_rows, train_embed, lib_embed, labels, prior_draws, noise_draws,
    coefficients, velocity, library_prior,
):
    steps, batch = batch_rows.shape
    O = batch // (B * T)
    R, D = train_embed.shape
    COLS = coefficients.shape[0]
    CP = -(-COLS // 16) * 16
    LQ = lib_embed.shape[0]
    OL = LQ // T
    Q = T * O
    vmem = lambda *shape, dtype=f32: pltpu.VMEM(shape, dtype)
    dma = lambda *shape: pltpu.SemaphoreType.DMA(shape)
    whole = pl.BlockSpec(memory_space=pltpu.VMEM)
    far = pl.BlockSpec(memory_space=pl.ANY)
    scratch = [
        vmem(R, D, dtype=bf16), vmem(LQ, D, dtype=bf16), vmem(1, R), vmem(COLS - 1, R),
        vmem(COLS - 1, R), vmem(COLS, R), vmem(COLS, R), vmem(COLS, R), vmem(COLS, R),
        vmem(R, 128), vmem(B * O, R, dtype=bf16), vmem(B * O, R, dtype=bf16),
        vmem(CP, R), vmem(CP, R), vmem(CP, R, dtype=bf16), vmem(CP, R, dtype=bf16),
        vmem(2, T, O, D, dtype=bf16), vmem(D, Q, dtype=bf16), vmem(CP, Q), vmem(CP, LQ),
        vmem(B * O, D, dtype=bf16), vmem(B * O, D, dtype=bf16),
        vmem(B * O, Q, dtype=bf16), vmem(B * O, LQ, dtype=bf16), vmem(B * O, LQ, dtype=bf16),
        vmem(B * O, O, dtype=bf16), vmem(2, CP, O),
        vmem(2, T, CP, O, dtype=bf16), vmem(2, T - 1, CP, O, dtype=bf16),
        vmem(T, CP, OL, dtype=bf16), vmem(T - 1, CP, OL, dtype=bf16),
        vmem(2, B, CP, O, dtype=bf16), vmem(2, CP, B * O, dtype=bf16),
        dma(7), dma(2), dma(2, T), dma(2, T), dma(2, T), dma(2, T),
        dma(3, T), dma(3, T), dma(2, B), dma(2, B),
    ]
    pairs = (2 * Q + LQ) * R
    return pl.pallas_call(
        functools.partial(body, T, B, COLS),
        out_shape=(
            jax.ShapeDtypeStruct((COLS, R), f32),
            jax.ShapeDtypeStruct((COLS, R), f32),
            jax.ShapeDtypeStruct((COLS, OL), f32),
        ),
        in_specs=[whole] + [far] * 7 + [whole],
        out_specs=(far, far, whole),
        scratch_shapes=scratch,
        compiler_params=pltpu.CompilerParams(
            collective_id=0, has_side_effects=True, vmem_limit_bytes=56 * 1024 * 1024
        ),
        cost_estimate=pl.CostEstimate(
            flops=2 * pairs * (D + COLS), bytes_accessed=8 * 1024 * 1024, transcendentals=2 * pairs
        ),
    )(
        batch_rows.reshape(steps * B * T, O), train_embed, lib_embed, labels[None, :],
        prior_draws, noise_draws, coefficients, velocity, library_prior,
    )


def solution(mesh):
    return jax.shard_map(
        functools.partial(per_device, mesh.shape["train"], mesh.shape["batch"]),
        mesh=mesh,
        in_specs=(
            P(),
            P("train", None),
            P("batch", None),
            P("train"),
            P(None, "train"),
            P(None, "train"),
            P(None, "train"),
            P(None, "train"),
            P(None, ("batch", "train")),
        ),
        out_specs=(P(None, "train"), P(None, "train"), P(None, ("batch", "train"))),
        check_vma=False,
    )
```

profile of v0, /device:TPU:0, one launch (start us, length us, event | category | flops | bytes accessed | tf_op | source)
XLA Modules:
  0.0 68.4 jit_solution(14600672858407469605)
XLA Ops:
  0.6 1.4 %reshape.9.rows_ref = s32[64,128]{1,0:T(8,128)} reshape(s32[2,4096]{1,0:T(2,128)} %param.9) | data formatting | bytes 65536 | tf_op jit(solution)/shard_map/reshape | solution.py:380
  2.0 61.8 %shard_map.112 = (f32[33,4096]{1,0:T(8,128)}, f32[33,4096]{1,0:T(8,128)}, f32[33,128]{1,0:T(8,128)}) custom-call(s32[64,128]{1,0:T(8,128)} %reshape.9.rows_ref, bf16[4096,256]{1,0:T(8,128)(2,1)} %embed_hbm.1, bf16[1024,256]{1,0:T(8,128)(2,1)} %lib_hbm.1, f32[1,4096]{1,0:T(1,128)} %bitcast.1, f32[32,4096]{1,0:T(8,128)} %prior_hbm.1, f32[32,4096]{1,0:T(8,128)} %noise_hbm.1, ...), custom_call_target="tpu_custom_call" | custom-call | flops 7272923136 | bytes 8388608 | tf_op jit(solution)/shard_map/pallas_call | solution.py:363
  63.9 0.0 copy-start
  63.9 2.0 %copy.15 = f32[33,4096]{1,0:T(8,128)} copy(f32[33,4096]{1,0:T(8,128)} %get-tuple-element.6) | data formatting | bytes 1081344
  65.8 2.0 %copy.16 = f32[33,4096]{1,0:T(8,128)} copy(f32[33,4096]{1,0:T(8,128)} %get-tuple-element.7) | data formatting | bytes 1081344
  67.8 0.0 copy-done
  67.8 0.6 copy.17
Async XLA Ops:
  63.9 4.0 %copy-start = (f32[33,128]{1,0:T(8,128)S(1)}, f32[33,128]{1,0:T(8,128)}, u32[]{:S(2)}) copy-start(f32[33,128]{1,0:T(8,128)} %get-tuple-element.8) | copy-start | bytes 50692
where the time goes:
time: 68.7 us; the launch traced here: 68.4 us
  Pallas kernels  61.8 us (90%)
  local copies, waits for them, and re-layouts  5.95 us (9%)
    pallas_call x1, Pallas kernels, per_device(): pl.pallas_call(functools.partial(body, T, B, COLS), out_shape=(jax.ShapeD...  61.8 us
    unnamed x5, local copies, waits for them, and re-layouts  4.55 us
    reshape x1, local copies, waits for them, and re-layouts, per_device(): batch_rows.reshape(steps * B * T, O)  1.4 us

commit v1 on v0

--- a/solution.py
+++ b/solution.py
@@ -16,7 +16,8 @@
 
 f32 = jnp.float32
 bf16 = jnp.bfloat16
-BLOCK = 256
+BLOCK = 1024
+NORM_BLOCK = 256
 
 
 def dot(a, b):
@@ -29,7 +30,7 @@
 
 def body(
     T, B, COLS,
-    rows_ref, embed_hbm, lib_hbm, labels_hbm, prior_hbm, noise_hbm, coef_hbm, vel_hbm, shift_ref,
+    rows_ref, embed_hbm, lib_hbm, labels_hbm, prior_hbm, noise_hbm, coef_hbm, vel_hbm,
     newc_hbm, newv_hbm, pred_ref,
     embed, lib, labels, prior, noise, coef, vel, outc, outv,
     norms, hot0, hot1, wide, targets, w_first, w_base,
@@ -46,7 +47,6 @@
     H = T // 2
     hots = (hot0, hot1)
     alpha = math.sqrt(5.0 / (length_sq * D))
-    gamma = alpha * math.log2(math.e)
     c1 = 1.5 / alpha
     c2 = 0.75 / (alpha * alpha)
     kappa = alpha * alpha / 3.0
@@ -75,14 +75,19 @@
         )
 
     base_row = (t * R).astype(f32)
-    diagonal = lax.broadcasted_iota(jnp.int32, (O, O), 0) == lax.broadcasted_iota(
-        jnp.int32, (O, O), 1
-    )
+    span = max(O, 128)
+    slots = lax.broadcasted_iota(jnp.int32, (O, span), 0)
+    lanes = lax.broadcasted_iota(jnp.int32, (O, span), 1)
 
     def build_hot(s, d):
         group = lax.rem(b + B - d, B)
-        run = rows_ref[pl.ds(s * (B * T) + group * T + t, 1), :].astype(f32) - base_row
-        column = jnp.sum(jnp.where(diagonal, run, 0.0), axis=1, keepdims=True).astype(jnp.int32)
+        first = (group * T + t) * O
+        chunk = first // span
+        run = rows_ref[s : s + 1, pl.ds(pl.multiple_of(chunk * span, span), span)]
+        picked = lanes == slots + (first - chunk * span)
+        column = jnp.sum(
+            jnp.where(picked, run.astype(f32) - base_row, 0.0), axis=1, keepdims=True
+        ).astype(jnp.int32)
         lane = lax.broadcasted_iota(jnp.int32, (O, R), 1)
         hots[s][d * O : (d + 1) * O, :] = jnp.where(column == lane, 1.0, 0.0).astype(bf16)
 
@@ -149,12 +154,12 @@
     send_queries(0)
 
     def norm_block(i, _):
-        at = pl.ds(pl.multiple_of(i * BLOCK, BLOCK), BLOCK)
+        at = pl.ds(pl.multiple_of(i * NORM_BLOCK, NORM_BLOCK), NORM_BLOCK)
         x = embed[at, :].astype(f32)
-        norms[at, :] = jnp.broadcast_to(jnp.sum(x * x, axis=1, keepdims=True), (BLOCK, 128))
+        norms[at, :] = jnp.broadcast_to(jnp.sum(x * x, axis=1, keepdims=True), (NORM_BLOCK, 128))
         return 0
 
-    lax.fori_loop(0, R // BLOCK, norm_block, 0)
+    lax.fori_loop(0, R // NORM_BLOCK, norm_block, 0)
 
     ins[2].wait()
     ins[3].wait()
@@ -173,7 +178,7 @@
         dist = jnp.maximum(dot(keys, qt[...]) + query_norms + wide_norms, 1e-20)
         root = dist * lax.rsqrt(dist)
         shifted = root + c1
-        return ((shifted * shifted + c2) * jnp.exp2(root * (-gamma))).astype(bf16)
+        return ((shifted * shifted + c2) * jnp.exp(root * (-alpha))).astype(bf16)
 
     def apply_blocks(lower, upper, weights, query_norms, total):
         def step(i, _):
@@ -318,13 +323,19 @@
     out_c.start()
     out_v.start()
 
-    total = scatter_recv(2)
-    pred_ref[0:1, :] = total[0:1]
-    pred_ref[1:COLS, :] = total[1:COLS] + shift_ref[...]
+    pred_ref[...] = scatter_recv(2)[0:COLS]
     out_c.wait()
     out_v.wait()
     for copy in sends:
         copy.wait_send()
+
+
+def finish(c_ref, v_ref, total_ref, shift_ref, newc_ref, newv_ref, pred_ref):
+    newc_ref[...] = c_ref[...]
+    newv_ref[...] = v_ref[...]
+    total = total_ref[...]
+    pred_ref[0:1, :] = total[0:1]
+    pred_ref[1:, :] = total[1:] + shift_ref[...]
 
 
 def per_device(
@@ -360,14 +371,15 @@
         dma(3, T), dma(3, T), dma(2, B), dma(2, B),
     ]
     pairs = (2 * Q + LQ) * R
-    return pl.pallas_call(
+    out_shape = (
+        jax.ShapeDtypeStruct((COLS, R), f32),
+        jax.ShapeDtypeStruct((COLS, R), f32),
+        jax.ShapeDtypeStruct((COLS, OL), f32),
+    )
+    parts = pl.pallas_call(
         functools.partial(body, T, B, COLS),
-        out_shape=(
-            jax.ShapeDtypeStruct((COLS, R), f32),
-            jax.ShapeDtypeStruct((COLS, R), f32),
-            jax.ShapeDtypeStruct((COLS, OL), f32),
-        ),
-        in_specs=[whole] + [far] * 7 + [whole],
+        out_shape=out_shape,
+        in_specs=[whole] + [far] * 7,
         out_specs=(far, far, whole),
         scratch_shapes=scratch,
         compiler_params=pltpu.CompilerParams(
@@ -377,9 +389,16 @@
             flops=2 * pairs * (D + COLS), bytes_accessed=8 * 1024 * 1024, transcendentals=2 * pairs
         ),
     )(
-        batch_rows.reshape(steps * B * T, O), train_embed, lib_embed, labels[None, :],
-        prior_draws, noise_draws, coefficients, velocity, library_prior,
+        batch_rows, train_embed, lib_embed, labels[None, :],
+        prior_draws, noise_draws, coefficients, velocity,
     )
+    return pl.pallas_call(
+        finish,
+        out_shape=out_shape,
+        in_specs=[whole] * 4,
+        out_specs=(whole, whole, whole),
+        compiler_params=pltpu.CompilerParams(vmem_limit_bytes=16 * 1024 * 1024),
+    )(*parts, library_prior)
 
 
 def solution(mesh):

time: 68.7 us -> 59.7 us (0.87)
  Pallas kernels: 61.8 us -> 55.8 us
  local copies, waits for them, and re-layouts: 5.95 us -> 2.9 us
    pallas_call x1 -> x2, Pallas kernels: 61.8 us -> 55.8 us  [the longest x1 54.6 us: per_device(): pl.pallas_call(functools.partial(body, T, B, COLS), out_shape=out_shape,...]
    unnamed x5 -> x8, local copies, waits for them, and re-layouts: 4.55 us -> 2.9 us
    reshape x1 -> x0, local copies, waits for them, and re-layouts: 1.4 us -> none  [per_device(): batch_rows.reshape(steps * B * T, O)]
where the time goes in v1:
time: 59.7 us; the launch traced here: 59.3 us
  Pallas kernels  55.8 us (93%)
  local copies, waits for them, and re-layouts  2.9 us (5%)
  between operations  0.67 us (1%)
    pallas_call x1, Pallas kernels, per_device(): pl.pallas_call(functools.partial(body, T, B, COLS), out_shape=out_shape,...  54.6 us
    unnamed x8, local copies, waits for them, and re-layouts  2.9 us

profile of v1, /device:TPU:0, one launch (start us, length us, event | category | flops | bytes accessed | tf_op | source)
XLA Modules:
  0.0 59.3 jit_solution(3446906550432480630)
XLA Ops:
  0.6 0.0 copy-start.3
  0.6 54.6 %shard_map.112 = (f32[33,4096]{1,0:T(8,128)}, f32[33,4096]{1,0:T(8,128)}, f32[33,128]{1,0:T(8,128)}) custom-call(s32[2,4096]{1,0:T(2,128)} %rows_ref.1, bf16[4096,256]{1,0:T(8,128)(2,1)} %embed_hbm.1, bf16[1024,256]{1,0:T(8,128)(2,1)} %lib_hbm.1, f32[1,4096]{1,0:T(1,128)} %bitcast.1, f32[32,4096]{1,0:T(8,128)} %prior_hbm.1, f32[32,4096]{1,0:T(8,128)} %noise_hbm.1, ...), custom_call_target="tpu_custom_call" | custom-call | flops 7272923136 | bytes 8388608 | tf_op jit(solution)/shard_map/pallas_call | solution.py:379
  55.3 0.0 copy-done.3
  55.3 0.0 copy-start
  55.3 1.1 %copy-done = f32[33,4096]{1,0:T(8,128)S(1)} copy-done((f32[33,4096]{1,0:T(8,128)S(1)}, f32[33,4096]{1,0:T(8,128)}, u32[]{:S(2)}) %copy-start) | copy-done | bytes 540696
  56.4 0.0 copy-start.1
  56.4 1.1 %copy-done.1 = f32[33,4096]{1,0:T(8,128)S(1)} copy-done((f32[33,4096]{1,0:T(8,128)S(1)}, f32[33,4096]{1,0:T(8,128)}, u32[]{:S(2)}) %copy-start.1) | copy-done | bytes 540696
  57.4 0.0 copy-start.2
  57.4 0.7 %copy-done.2 = f32[33,128]{1,0:T(8,128)S(1)} copy-done((f32[33,128]{1,0:T(8,128)S(1)}, f32[33,128]{1,0:T(8,128)}, u32[]{:S(2)}) %copy-start.2) | copy-done | bytes 16920
  58.2 1.1 %shard_map.113 = (f32[33,4096]{1,0:T(8,128)}, f32[33,4096]{1,0:T(8,128)}, f32[33,128]{1,0:T(8,128)}) custom-call(f32[33,4096]{1,0:T(8,128)S(1)} %copy-done, f32[33,4096]{1,0:T(8,128)S(1)} %copy-done.1, f32[33,128]{1,0:T(8,128)S(1)} %copy-done.2, f32[32,128]{1,0:T(8,128)S(1)} %copy-done.3), custom_call_target="tpu_custom_call" | custom-call | tf_op jit(solution)/shard_map/pallas_call | solution.py:395
Async XLA Ops:
  0.6 54.6 %copy-start.3 = (f32[32,128]{1,0:T(8,128)S(1)}, f32[32,128]{1,0:T(8,128)}, u32[]{:S(2)}) copy-start(f32[32,128]{1,0:T(8,128)} %shift_ref.1) | copy-start | bytes 49156
  55.3 1.1 %copy-start = (f32[33,4096]{1,0:T(8,128)S(1)}, f32[33,4096]{1,0:T(8,128)}, u32[]{:S(2)}) copy-start(f32[33,4096]{1,0:T(8,128)} %get-tuple-element.6.c_ref) | copy-start | bytes 1622020
  56.4 1.1 %copy-start.1 = (f32[33,4096]{1,0:T(8,128)S(1)}, f32[33,4096]{1,0:T(8,128)}, u32[]{:S(2)}) copy-start(f32[33,4096]{1,0:T(8,128)} %get-tuple-element.7.v_ref) | copy-start | bytes 1622020
  57.4 0.7 %copy-start.2 = (f32[33,128]{1,0:T(8,128)S(1)}, f32[33,128]{1,0:T(8,128)}, u32[]{:S(2)}) copy-start(f32[33,128]{1,0:T(8,128)} %get-tuple-element.8.total_ref) | copy-start | bytes 50692
